TPU v7x, 256 devices: a whole 4x4x8 slice. The times are simulated.
256 devices in a mesh: dp: 32 (over x_hi, z, core), row: 2 (over x_lo), col: 4 (over y).
Axes of the slice: x: 4 (x_hi: 2, x_lo: 2; x = x_hi * 2 + x_lo), y: 4, z: 8, core: 2. Of those that a mesh axis runs over, the one named last changes fastest.
Arguments:
- out_grads: bfloat16 [40960, 4096], P('dp', 'row'), may hold values from -0.0546875 to 0.0546875
- activations: bfloat16 [40960, 4096], P('dp', 'col'), may hold values from -6 to 6
- output_factor: bfloat16 [2, 2048, 4096], P('row', 'dp'), may hold values from -1 to 4
- input_factor: bfloat16 [4096, 4096], P('col', ('dp', 'row')), may hold values from -1 to 4, as said below
Outputs:
- preconditioned: bfloat16 [4096, 4096], P('row', 'col')
Inputs may be any that keep to these rules, and one draw needn't show every extreme that they name: input_factor is symmetric: entry (i, j) equals entry (j, i); and output_factor, read as a [4096, 4096] matrix (its first two dimensions joined in order), is symmetric too.
All inputs are finite; a program needn't handle non-finite values.
Results may differ from a plain program's by a relative error of at most 0.028.
Values may be sent and summed in bfloat16 or wider, within the bound.
A program may use at most 64 MiB of HBM per device.

v0:
```python
import jax
import jax.numpy as jnp
from jax import lax
from jax.sharding import PartitionSpec as P


def shards(out_grads, activations, output_factor, input_factor):
    summed = lax.psum_scatter(
        lax.dot_general(
            out_grads, activations, (((0,), (0,)), ((), ())), preferred_element_type=jnp.float32
        ).astype(jnp.bfloat16),
        "dp",
        scatter_dimension=0,
        tiled=True,
    )
    partial_terms = jnp.dot(
        summed,
        lax.all_gather(input_factor, ("dp", "row"), axis=1, tiled=True),
        preferred_element_type=jnp.float32,
    )
    hidden = lax.psum_scatter(
        partial_terms.astype(jnp.bfloat16), "col", scatter_dimension=1, tiled=True
    )
    block = lax.all_gather(hidden, "dp", axis=0, tiled=True)
    factor_here = output_factor[0]
    product = jnp.dot(
        factor_here,
        lax.all_gather(block, "row", axis=0, tiled=True),
        preferred_element_type=jnp.float32,
    )
    result = product.astype(jnp.bfloat16)
    return lax.all_gather(result, "dp", axis=0, tiled=True)


def solution(mesh):
    placed = (P("dp", "row"), P("dp", "col"), P("row", "dp", None), P("col", ("dp", "row")))
    return jax.shard_map(
        shards, mesh=mesh, in_specs=placed, out_specs=P("row", "col"), check_vma=False
    )
```

profile of v0, /device:TPU:1, one launch (start us, length us, event | category | flops | bytes accessed | tf_op | source)
XLA Modules:
  0.0 564.0 jit_solution(1314360196383419162)
XLA Ops:
  7.4 0.0 copy-start
  7.4 1.7 copy-done
  9.1 9.7 %convolution_convert_fusion.1 = bf16[2048,1024]{1,0:T(8,128)(2,1)} fusion(bf16[1280,2048]{1,0:T(8,128)(2,1)} %param.4, bf16[1280,1024]{1,0:T(8,128)(2,1)S(1)} %copy-done), kind=kOutput, calls=%fused_computation.1 | convolution fusion | flops 5370806272 | bytes 12058624 | tf_op jit(solution)/shard_map/dot_general | solution.py:9
  18.8 0.0 reduce-scatter.3.cloned.1.call-update
  18.8 0.0 all-gather.5.cloned.1.call-start
  18.9 0.5 all-gather.5.cloned.1.call-update
  19.4 0.0 copy-start.1
  19.4 0.0 reduce-scatter.5.cloned.1.call-start
  19.5 127.2 %reduce-scatter.3.cloned.1.call-done = bf16[64,1024]{1,0:T(8,128)(2,1)} async-done(((bf16[2048,1024]{1,0:T(8,128)(2,1)}), bf16[64,1024]{1,0:T(8,128)(2,1)}) %reduce-scatter.3.cloned.1.call-update) | async-done | bytes 131088 | tf_op jit(solution)/shard_map/reduce_scatter | solution.py:8
  146.7 72.0 %all-gather.5.cloned.1.call-done = bf16[1024,4096]{0,1:T(8,128)(2,1)} async-done(((bf16[1024,64]{0,1:T(8,128)(2,1)}), bf16[1024,4096]{0,1:T(8,128)(2,1)}) %all-gather.5.cloned.1.call-update) | async-done | bytes 8388624 | tf_op jit(solution)/shard_map/all_gather | solution.py:18
  218.7 6.9 %convolution_convert_fusion = bf16[64,4096]{1,0:T(8,128)(2,1)} fusion(bf16[64,1024]{1,0:T(8,128)(2,1)} %reduce-scatter.3.cloned.1.call-done, bf16[1024,4096]{0,1:T(8,128)(2,1)} %all-gather.5.cloned.1.call-done), kind=kOutput, calls=%fused_computation | convolution fusion | flops 537133056 | bytes 9043968 | tf_op jit(solution)/shard_map/dot_general | solution.py:16
  225.6 0.0 reduce-scatter.5.cloned.1.call-update
  225.6 0.0 all-gather.7.cloned.1.call-start
  225.7 33.6 %reduce-scatter.5.cloned.1.call-done = bf16[64,1024]{1,0:T(8,128)(2,1)} async-done(((bf16[64,4096]{1,0:T(8,128)(2,1)}), bf16[64,1024]{1,0:T(8,128)(2,1)}) %reduce-scatter.5.cloned.1.call-update) | async-done | bytes 131088 | tf_op jit(solution)/shard_map/reduce_scatter | solution.py:21
  259.2 0.0 all-gather.7.cloned.1.call-update
  259.2 0.0 all-gather.9.cloned.1.call-start
  259.3 91.8 %all-gather.7.cloned.1.call-done = bf16[2048,1024]{1,0:T(8,128)(2,1)} async-done(((bf16[64,1024]{1,0:T(8,128)(2,1)}), bf16[2048,1024]{1,0:T(8,128)(2,1)}) %all-gather.7.cloned.1.call-update) | async-done | bytes 4194320 | tf_op jit(solution)/shard_map/all_gather | solution.py:24
  351.1 0.0 all-gather.9.cloned.1.call-update
  351.1 0.0 all-gather.11.cloned.1.call-start
  351.1 107.1 %all-gather.9.cloned.1.call-done = bf16[4096,1024]{1,0:T(8,128)(2,1)} async-done(((bf16[2048,1024]{1,0:T(8,128)(2,1)}), bf16[4096,1024]{1,0:T(8,128)(2,1)}) %all-gather.9.cloned.1.call-update) | async-done | bytes 8388624 | tf_op jit(solution)/shard_map/all_gather | solution.py:28
  458.2 5.6 fusion
  463.8 0.0 all-gather.11.cloned.1.call-update
  463.9 88.4 %all-gather.11.cloned.1.call-done = bf16[2048,1024]{1,0:T(8,128)(2,1)} async-done(((bf16[64,1024]{1,0:T(8,128)(2,1)}), bf16[2048,1024]{1,0:T(8,128)(2,1)}) %all-gather.11.cloned.1.call-update) | async-done | bytes 4194320 | tf_op jit(solution)/shard_map/all_gather | solution.py:32
  552.3 4.6 copy.6
  (2 shorter events, 0.0 us)
Async XLA Ops:
  7.4 1.7 copy-start
  7.4 139.3 %reduce-scatter.3.cloned.1.call-start = ((), (), s32[]{:S(2)}) async-start(), calls=%async_computation.2 | async-start | bytes 4325376 | tf_op jit(solution)/shard_map/reduce_scatter | solution.py:8
  18.8 199.8 %all-gather.5.cloned.1.call-start = ((), (), s32[]{:S(2)}) async-start(), calls=%async_computation.3 | async-start | bytes 8519680 | tf_op jit(solution)/shard_map/all_gather | solution.py:18
  19.4 438.8 %copy-start.1 = (bf16[1,64,4096]{2,1,0:T(8,128)(2,1)S(1)}, bf16[1,64,4096]{2,1,0:T(8,128)(2,1)}, u32[]{:S(2)}) copy-start(bf16[1,64,4096]{2,1,0:T(8,128)(2,1)} %param.6) | copy-start | bytes 1572868
  19.4 239.8 %reduce-scatter.5.cloned.1.call-start = ((), (), s32[]{:S(2)}) async-start(), calls=%async_computation.4 | async-start | bytes 655360 | tf_op jit(solution)/shard_map/reduce_scatter | solution.py:21
  225.6 125.5 %all-gather.7.cloned.1.call-start = ((), (), s32[]{:S(2)}) async-start(), calls=%async_computation.5 | async-start | bytes 4325376 | tf_op jit(solution)/shard_map/all_gather | solution.py:24
  259.2 199.0 %all-gather.9.cloned.1.call-start = ((), (), s32[]{:S(2)}) async-start(), calls=%async_computation.6 | async-start | bytes 12582912 | tf_op jit(solution)/shard_map/all_gather | solution.py:28
  351.1 201.2 %all-gather.11.cloned.1.call-start = ((), (), s32[]{:S(2)}) async-start(), calls=%async_computation.7 | async-start | bytes 4325376 | tf_op jit(solution)/shard_map/all_gather | solution.py:32
Sparse Core Ops, SparseCore 0:
  19.0 127.6 reduce-scatter.2
  225.7 33.4 reduce-scatter.4
  262.4 88.6 all-gather.6
  352.9 105.3 all-gather.8
  464.0 88.2 all-gather.10
Sparse Core Ops, SparseCore 1:
  21.3 197.3 all-gather.4
where the time goes:
time: 564 us
  waiting for transfers between devices  521 us (92%)
  matrix products  22.2 us (4%)
  between operations  14.6 us (3%)
  local copies, waits for them, and re-layouts  6.38 us (1%)
    reduce_scatter x1, waiting for transfers between devices, shards(): lax.psum_scatter(lax.dot_general(out_grads, activations, (((0,), (0,)), (...  127 us
    all_gather x1, waiting for transfers between devices, shards(): lax.all_gather(block, 'row', axis=0, tiled=True)  107 us
    all_gather x1, waiting for transfers between devices, shards(): block = lax.all_gather(hidden, 'dp', axis=0, tiled=True)  91.8 us
    all_gather x1, waiting for transfers between devices, shards(): return lax.all_gather(result, 'dp', axis=0, tiled=True)  88.4 us
    all_gather x1, waiting for transfers between devices, shards(): lax.all_gather(input_factor, ('dp', 'row'), axis=1, tiled=True)  72 us
    reduce_scatter x1, waiting for transfers between devices, shards(): lax.psum_scatter(partial_terms.astype(jnp.bfloat16), 'col', scatter_dimen...  33.6 us
  transfers between devices with their start and end apart: 6, of which 6 were waited for; matrix products, arithmetic and copies ran while one was open for 0% of the time, Pallas kernels for 0%

commit v1 on v0

v1 whole, which is shorter than its diff:
```python
import functools

import jax
import jax.numpy as jnp
from jax import lax
from jax.experimental import pallas as pl
from jax.experimental.pallas import tpu as pltpu
from jax.sharding import PartitionSpec as P

NX, NY, NZ = 4, 4, 8
BF16, F32 = jnp.bfloat16, jnp.float32
COPIES = 192


def kernel(
    g_hbm, a_hbm, l_hbm, r_hbm, out,
    g_v, a_v, own, give, take, ring_s, ring_r, xs, xr, gt, lbuf, rbuf, r_mine, mbuf, pf, ring2_s, ring2_r,
    load_sem, send_sem, recv_sem, r_send, r_recv,
):
    d, row, y = lax.axis_index("dp"), lax.axis_index("row"), lax.axis_index("col")
    k, z, xh = d % 2, (d // 2) % NZ, d // (2 * NZ)
    x = 2 * xh + row

    def device(x, y, z, k):
        return {"dp": (x // 2) * (2 * NZ) + z * 2 + k, "row": x % 2, "col": y}

    def at_x(n, core=None):
        return device((x + n) % NX, y, z, k if core is None else core)

    def at_y(n):
        return device(x, (y + n) % NY, z, k)

    def at_z(n):
        return device(x, y, (z + n) % NZ, k)

    sibling = device(x, y, z, 1 - k)
    count = [0]
    sent = []

    def send(src, dst, target):
        i = count[0]
        count[0] += 1
        copy = pltpu.make_async_remote_copy(
            src_ref=src, dst_ref=dst, send_sem=send_sem.at[i], recv_sem=recv_sem.at[i],
            device_id=target, device_id_type=pl.DeviceIdType.MESH,
        )
        copy.start()
        sent.append(copy)
        return copy

    loads = []

    def load(src, dst):
        copy = pltpu.make_async_copy(src, dst, load_sem.at[len(loads)])
        copy.start()
        loads.append(copy)
        return copy

    home = z // 4
    load_l = [load(l_hbm.at[0, :, pl.ds(q * 1024, 1024)], lbuf.at[q, z]) for q in range(4)]
    load_r = load(r_hbm, r_mine)
    load_a = load(a_hbm, a_v)
    load_g = load(g_hbm, g_v)

    barrier = pltpu.get_barrier_semaphore()
    partners = [at_z(1), at_z(-1), at_z(4), sibling] + [at_y(n) for n in (1, 2, 3)]
    partners += [at_x(n, core) for n in (1, 2, 3) for core in (k, 1 - k)]
    for partner in partners:
        pl.semaphore_signal(barrier, inc=1, device_id=partner, device_id_type=pl.DeviceIdType.MESH)
    pl.semaphore_wait(barrier, len(partners))

    for copy in load_l:
        copy.wait()
    load_r.wait()

    l_from = {}

    def l_block(q, n):
        return lbuf.at[q, (z + n) % NZ]

    def l_half(q, n, half):
        return lbuf.at[q, (z + n) % NZ, pl.ds(32 * half, 32)]

    def l_z(step):
        if step == 0:
            for sign in (1, -1):
                l_from[sign, 1] = send(l_block(y, 0), l_block(y, 0), at_z(sign))
            return
        for sign in (1, -1):
            l_from[sign, step].wait_recv()
            n = -sign * step
            if step < 3:
                l_from[sign, step + 1] = send(l_block(y, n), l_block(y, n), at_z(sign))
            elif step == 3:
                half = 0 if sign == 1 else 1
                l_from[sign, 4] = send(l_half(y, n, half), l_half(y, n, half), at_z(sign))
        for n in ((-step, step) if step < 4 else (4,)):
            for sign in (1, -1):
                l_from["y", sign, n] = send(l_block(y, n), l_block(y, n), at_y(sign))

    def l_y(*offsets):
        for n in offsets:
            for sign in (1, -1):
                l_from["y", sign, n].wait_recv()
                half = 0 if sign == 1 else 1
                block = l_half((y + NY - sign) % NY, n, half)
                l_from["f", sign, n] = send(block, block, at_y(sign))

    def r_copy(src, dst, i, target):
        return pltpu.make_async_remote_copy(
            src_ref=src, dst_ref=dst, send_sem=r_send.at[i], recv_sem=r_recv.at[i],
            device_id=target, device_id_type=pl.DeviceIdType.MESH,
        )

    away = r_copy(r_mine, rbuf.at[2 * xh + home, row], 0, at_z(4))

    @pl.when(k != home)
    def _():
        away.start()

    pair = rbuf.at[pl.ds(2 * xh, 2), row]
    spread = [r_copy(pair, pair, 1 + n, at_x(n)) for n in (1, 2, 3)]
    spread += [r_copy(pair, pair, 5 + n, at_x(n, 1 - k)) for n in (0, 1, 2, 3)]

    def r_x():
        @pl.when(k == home)
        def _():
            rbuf[2 * xh + home, row] = r_mine[...]
            away.wait_recv()
            for copy in spread:
                copy.start()

    def r_end():
        @pl.when(k == home)
        def _():
            for copy in spread[:3]:
                copy.wait_recv()
            for copy in spread:
                copy.wait_send()

        @pl.when(k != home)
        def _():
            away.wait_send()
            for copy in spread[3:]:
                copy.wait_recv()

    l_z(0)

    exchange = {}

    def term(q_off):
        q = (z + q_off) % 4
        a_part = a_v[:, pl.ds(pl.multiple_of(q * 256, 256), 256)]

        def part(core, n):
            start = pl.multiple_of(core * 1024 + n * 512, 512)
            return lax.dot_general(
                a_part, g_v[:, pl.ds(start, 512)], (((0,), (0,)), ((), ())), preferred_element_type=F32
            )

        for n in range(2):
            give[q, :, n * 512:(n + 1) * 512] = part(1 - k, n).astype(BF16)
        exchange[q_off] = send(give.at[q], take.at[q], sibling)
        for n in range(2):
            own[q, :, n * 512:(n + 1) * 512] = part(k, n)

    def chip_term(n, h):
        chunk = (z + n) % NZ
        rows = pl.ds(pl.multiple_of((chunk // 4) * 128 + h * 64, 64), 64)
        return own[chunk % 4, rows, :] + take[chunk % 4, rows, :].astype(F32)

    def partial(n, h):
        return pf[(z + n) % NZ, h * 32:(h + 1) * 32, :]

    def ring_step(step, mine, buf_s, buf_r, arrived):
        for h, side in ((0, 0), (1, 1), (1, 0), (0, 1)):
            sign = 1 - 2 * side
            if step == 0 and h != side:
                continue
            total = mine(sign * (4 - step), h)
            if (side, h) in arrived:
                arrived[side, h].wait_recv()
                total = total + buf_r[side, h, step - 1].astype(F32)
            buf_s[side, h, step] = total.astype(BF16)
            arrived[side, h] = send(buf_s.at[side, h, step], buf_r.at[side, h, step], at_z(sign))

    def ring_end(h, mine, buf_r, arrived):
        for side in (0, 1):
            arrived[side, h].wait_recv()
        return mine(0, h) + buf_r[0, h, 3].astype(F32) + buf_r[1, h, 3].astype(F32)

    load_a.wait()
    load_g.wait()
    arrived = {}
    term(0)
    term(3)
    exchange[0].wait_recv()
    ring_step(0, chip_term, ring_s, ring_r, arrived)
    term(1)
    l_z(1)
    exchange[3].wait_recv()
    exchange[1].wait_recv()
    ring_step(1, chip_term, ring_s, ring_r, arrived)
    term(2)
    r_x()
    l_z(2)
    exchange[2].wait_recv()
    ring_step(2, chip_term, ring_s, ring_r, arrived)
    l_z(3)
    ring_step(3, chip_term, ring_s, ring_r, arrived)
    l_y(-1, 1)
    l_z(4)

    other, same = 2 * (1 - row) + k, 2 * row + k
    from_x = {}
    for h in (0, 1):
        xs[h] = ring_end(h, chip_term, ring_r, arrived).astype(BF16)
        for side in (0, 1):
            from_x[side, h] = send(xs.at[h], xr.at[side, h], at_x(1 - 2 * side))
    l_y(-2, 2)
    halves, passed = {}, []
    for h in (0, 1):
        for side in (0, 1):
            from_x[side, h].wait_recv()
        rows = pl.ds(64 * h, 64)
        gt[other, rows, :] = (xr[0, h].astype(F32) + xr[1, h].astype(F32)).astype(BF16)
        for side in (0, 1):
            part = gt.at[other, pl.ds(64 * h + 32 * side, 32)]
            halves[side, h] = send(part, part, at_x(1 - 2 * side))
        passed.append(send(gt.at[other, rows], gt.at[other, rows], sibling))
    l_y(-3, 3)
    l_y(4)
    for h in (0, 1):
        for side in (0, 1):
            halves[side, h].wait_recv()
        rows = pl.ds(64 * h, 64)
        passed.append(send(gt.at[same, rows], gt.at[same, rows], sibling))
    for n in (-1, 1, -2, 2, -3, 3, 4):
        for sign in (1, -1):
            l_from["f", sign, n].wait_recv()
    for copy in passed:
        copy.wait_recv()

    left = jnp.zeros((128, 512), F32)
    for q in range(4):
        left = left + lax.dot_general(
            gt[q], lbuf[q].reshape(512, 1024), (((1,), (1,)), ((), ())), preferred_element_type=F32
        )
    mbuf[y] = left.astype(BF16)
    gathered = [send(mbuf.at[y], mbuf.at[y], at_y(n)) for n in (1, 3, 2)]
    r_end()
    for copy in gathered:
        copy.wait_recv()

    left_all = mbuf[...].reshape(512, 512)
    for n in range(2):
        right = rbuf[:, :, :, n * 512:(n + 1) * 512].reshape(512, 512)
        pf[:, :, n * 512:(n + 1) * 512] = lax.dot_general(
            left_all, right, (((0,), (0,)), ((), ())), preferred_element_type=F32
        ).reshape(8, 64, 512)
    arrived2 = {}
    for step in range(4):
        ring_step(step, partial, ring2_s, ring2_r, arrived2)

    def block(half, n, part=None):
        start = (half * NZ + (z + n) % NZ) * 128 + k * 64
        if part is not None:
            return out.at[pl.ds(pl.multiple_of(start + 32 * part, 32), 32)]
        return out.at[pl.ds(pl.multiple_of(start, 64), 64)]

    for h in (0, 1):
        start = pl.multiple_of((xh * NZ + z) * 128 + k * 64 + h * 32, 32)
        out[pl.ds(start, 32), :] = ring_end(h, partial, ring2_r, arrived2).astype(BF16)

    into, across = {}, []

    def start_block(half):
        for side in (0, 1):
            into[half, side, 1] = send(block(xhs[half], 0), block(xhs[half], 0), at_z(1 - 2 * side))
        across.append(send(block(xhs[half], 0), block(xhs[half], 0), sibling))

    xhs = (xh, 1 - xh)
    opposite = send(block(xh, 0), block(xh, 0), at_x(2))
    start_block(0)
    opposite.wait_recv()
    start_block(1)
    for step in range(1, 5):
        for half in (0, 1):
            for side in (0, 1):
                sign = 1 - 2 * side
                into[half, side, step].wait_recv()
                n = -sign * step
                if step < 3:
                    into[half, side, step + 1] = send(block(xhs[half], n), block(xhs[half], n), at_z(sign))
                elif step == 3:
                    into[half, side, 4] = send(block(xhs[half], n, side), block(xhs[half], n, side), at_z(sign))
                if step < 4:
                    across.append(send(block(xhs[half], n), block(xhs[half], n), sibling))
            if step == 4:
                across.append(send(block(xhs[half], 4), block(xhs[half], 4), sibling))
    for copy in across:
        copy.wait_recv()
    for copy in sent:
        copy.wait_send()
    assert count[0] <= COPIES, count[0]


def shards(out_grads, activations, output_factor, input_factor):
    vmem = pltpu.VMEM
    dma = pltpu.SemaphoreType.DMA
    anywhere = pl.BlockSpec(memory_space=pl.ANY)
    return pl.pallas_call(
        kernel,
        out_shape=jax.ShapeDtypeStruct((2048, 1024), BF16),
        in_specs=[anywhere] * 4,
        out_specs=pl.BlockSpec(memory_space=pltpu.VMEM),
        scratch_shapes=[
            vmem((1280, 2048), BF16),
            vmem((1280, 1024), BF16),
            vmem((4, 256, 1024), F32),
            vmem((4, 256, 1024), BF16),
            vmem((4, 256, 1024), BF16),
            vmem((2, 2, 4, 64, 1024), BF16),
            vmem((2, 2, 4, 64, 1024), BF16),
            vmem((2, 64, 1024), BF16),
            vmem((2, 2, 64, 1024), BF16),
            vmem((4, 128, 1024), BF16),
            vmem((4, 8, 64, 1024), BF16),
            vmem((4, 2, 64, 1024), BF16),
            vmem((64, 1024), BF16),
            vmem((4, 128, 512), BF16),
            vmem((8, 64, 1024), F32),
            vmem((2, 2, 4, 32, 1024), BF16),
            vmem((2, 2, 4, 32, 1024), BF16),
            dma((8,)), dma((COPIES,)), dma((COPIES,)), dma((9,)), dma((9,)),
        ],
        compiler_params=pltpu.CompilerParams(
            collective_id=0, has_side_effects=True, vmem_limit_bytes=56 * 2**20
        ),
    )(out_grads, activations, output_factor, input_factor.T)


def solution(mesh):
    placed = (P("dp", "row"), P("dp", "col"), P("row", "dp", None), P("col", ("dp", "row")))
    return jax.shard_map(
        shards, mesh=mesh, in_specs=placed, out_specs=P("row", "col"), check_vma=False
    )
```

time: 564 us -> 121 us (0.21)
  waiting for transfers between devices: 521 us -> 0 us
  Pallas kernels: 0 us -> 116 us
  matrix products: 22.2 us -> 0 us
  between operations: 14.6 us -> 0.01 us
    all_gather x4 -> x0, waiting for transfers between devices: 359 us -> none  [the longest x1 107 us: shards(): lax.all_gather(block, 'row', axis=0, tiled=True)]
    reduce_scatter x2 -> x0, waiting for transfers between devices: 161 us -> none  [the longest x1 127 us: shards(): lax.psum_scatter(lax.dot_general(out_grads, activations, (((0,), (0,)), (...]
    pallas_call x0 -> x1, Pallas kernels: none -> 116 us  [shards(): pl.pallas_call(kernel, out_shape=jax.ShapeDtypeStruct((2048, 1024), BF16)...]
    dot_general x3 -> x0, matrix products: 22.2 us -> none  [the longest x1 9.7 us: shards(): lax.dot_general(out_grads, activations, (((0,), (0,)), ((), ())), preferr...]
  transfers between devices with their start and end apart: 6 -> 0, of which waited for: 6 -> 0; matrix products, arithmetic and copies ran while one was open for 0% -> 0% of each run, Pallas kernels for 0% -> 0%
where the time goes in v1:
time: 121 us
  Pallas kernels  116 us (96%)
  local copies, waits for them, and re-layouts  4.64 us (4%)
    pallas_call x1, Pallas kernels, shards(): pl.pallas_call(kernel, out_shape=jax.ShapeDtypeStruct((2048, 1024), BF16)...  116 us
    unnamed x1, local copies, waits for them, and re-layouts  4.64 us

profile of v1, /device:TPU:1, one launch (start us, length us, event | category | flops | bytes accessed | tf_op | source)
XLA Modules:
  0.0 120.7 jit_solution(13000991456090307746)
XLA Ops:
  0.0 116.0 %shard_map.46 = bf16[2048,1024]{1,0:T(8,128)(2,1)} custom-call(bf16[1280,2048]{1,0:T(8,128)(2,1)} %g_hbm.1, bf16[1280,1024]{1,0:T(8,128)(2,1)} %a_hbm.1, bf16[1,64,4096]{2,1,0:T(8,128)(2,1)} %l_hbm.1, bf16[64,1024]{1,0:T(8,128)(2,1)} %bitcast.1), custom_call_target="tpu_custom_call" | custom-call | tf_op jit(solution)/shard_map/pallas_call | solution.py:312
  116.0 4.6 %copy.6 = bf16[2048,1024]{1,0:T(8,128)(2,1)} copy(bf16[2048,1024]{1,0:T(8,128)(2,1)} %shard_map.46) | data formatting | bytes 8388608

commit v2 on v1

--- a/solution.py
+++ b/solution.py
@@ -14,7 +14,7 @@
 
 def kernel(
     g_hbm, a_hbm, l_hbm, r_hbm, out,
-    g_v, a_v, own, give, take, ring_s, ring_r, xs, xr, gt, lbuf, rbuf, r_mine, mbuf, pf, ring2_s, ring2_r,
+    g_v, a_v, own, give, take, ring_s, ring_r, xs, xr, gt, lbuf, rbuf, r_mine, mbuf, pf, ring2_s, ring2_r, final,
     load_sem, send_sem, recv_sem, r_send, r_recv,
 ):
     d, row, y = lax.axis_index("dp"), lax.axis_index("row"), lax.axis_index("col")
@@ -57,21 +57,19 @@
         return copy
 
     home = z // 4
+    load_a = load(a_hbm, a_v)
+    load_g = []
+    for n in range(4):
+        part = pl.ds(pl.multiple_of((n // 2 + (1 - k)) % 2 * 1024 + n % 2 * 512, 512), 512)
+        load_g.append(load(g_hbm.at[:, part], g_v.at[:, part]))
     load_l = [load(l_hbm.at[0, :, pl.ds(q * 1024, 1024)], lbuf.at[q, z]) for q in range(4)]
     load_r = load(r_hbm, r_mine)
-    load_a = load(a_hbm, a_v)
-    load_g = load(g_hbm, g_v)
 
     barrier = pltpu.get_barrier_semaphore()
     partners = [at_z(1), at_z(-1), at_z(4), sibling] + [at_y(n) for n in (1, 2, 3)]
     partners += [at_x(n, core) for n in (1, 2, 3) for core in (k, 1 - k)]
     for partner in partners:
         pl.semaphore_signal(barrier, inc=1, device_id=partner, device_id_type=pl.DeviceIdType.MESH)
-    pl.semaphore_wait(barrier, len(partners))
-
-    for copy in load_l:
-        copy.wait()
-    load_r.wait()
 
     l_from = {}
 
@@ -87,15 +85,18 @@
                 l_from[sign, 1] = send(l_block(y, 0), l_block(y, 0), at_z(sign))
             return
         for sign in (1, -1):
-            l_from[sign, step].wait_recv()
             n = -sign * step
             if step < 3:
                 l_from[sign, step + 1] = send(l_block(y, n), l_block(y, n), at_z(sign))
             elif step == 3:
                 half = 0 if sign == 1 else 1
                 l_from[sign, 4] = send(l_half(y, n, half), l_half(y, n, half), at_z(sign))
+
+    def l_over_y(step):
+        for sign in (1, -1):
+            l_from[sign, step].wait_recv()
         for n in ((-step, step) if step < 4 else (4,)):
-            for sign in (1, -1):
+            for sign in ((1, -1) if step < 3 else (1, -1, 2)):
                 l_from["y", sign, n] = send(l_block(y, n), l_block(y, n), at_y(sign))
 
     def l_y(*offsets):
@@ -114,10 +115,6 @@
 
     away = r_copy(r_mine, rbuf.at[2 * xh + home, row], 0, at_z(4))
 
-    @pl.when(k != home)
-    def _():
-        away.start()
-
     pair = rbuf.at[pl.ds(2 * xh, 2), row]
     spread = [r_copy(pair, pair, 1 + n, at_x(n)) for n in (1, 2, 3)]
     spread += [r_copy(pair, pair, 5 + n, at_x(n, 1 - k)) for n in (0, 1, 2, 3)]
@@ -144,25 +141,28 @@
             for copy in spread[3:]:
                 copy.wait_recv()
 
-    l_z(0)
-
     exchange = {}
 
-    def term(q_off):
+    def term(q_off, core):
         q = (z + q_off) % 4
         a_part = a_v[:, pl.ds(pl.multiple_of(q * 256, 256), 256)]
 
-        def part(core, n):
-            start = pl.multiple_of(core * 1024 + n * 512, 512)
+        def part(half, n):
+            start = pl.multiple_of(half * 1024 + n * 512, 512)
             return lax.dot_general(
                 a_part, g_v[:, pl.ds(start, 512)], (((0,), (0,)), ((), ())), preferred_element_type=F32
             )
 
-        for n in range(2):
-            give[q, :, n * 512:(n + 1) * 512] = part(1 - k, n).astype(BF16)
+        if core == 0:
+            for n in range(2):
+                give[q, :, n * 512:(n + 1) * 512] = part(1 - k, n).astype(BF16)
+        else:
+            for n in range(2):
+                own[q, :, n * 512:(n + 1) * 512] = part(k, n)
+
+    def trade(q_off):
+        q = (z + q_off) % 4
         exchange[q_off] = send(give.at[q], take.at[q], sibling)
-        for n in range(2):
-            own[q, :, n * 512:(n + 1) * 512] = part(k, n)
 
     def chip_term(n, h):
         chunk = (z + n) % NZ
@@ -189,27 +189,50 @@
             arrived[side, h].wait_recv()
         return mine(0, h) + buf_r[0, h, 3].astype(F32) + buf_r[1, h, 3].astype(F32)
 
+    arrived = {}
     load_a.wait()
-    load_g.wait()
-    arrived = {}
-    term(0)
-    term(3)
+    for copy in load_g[:2]:
+        copy.wait()
+    term(0, 0)
+    for copy in load_l:
+        copy.wait()
+    load_r.wait()
+    pl.semaphore_wait(barrier, len(partners))
+    trade(0)
+    l_z(0)
+
+    @pl.when(k != home)
+    def _():
+        away.start()
+
+    for copy in load_g[2:]:
+        copy.wait()
+    term(0, 1)
+    term(3, 0)
+    trade(3)
     exchange[0].wait_recv()
     ring_step(0, chip_term, ring_s, ring_r, arrived)
-    term(1)
+    term(1, 0)
+    trade(1)
+    term(3, 1)
+    term(1, 1)
+    l_over_y(1)
     l_z(1)
     exchange[3].wait_recv()
     exchange[1].wait_recv()
     ring_step(1, chip_term, ring_s, ring_r, arrived)
-    term(2)
+    term(2, 0)
+    trade(2)
+    term(2, 1)
     r_x()
-    l_z(2)
+    l_over_y(2)
     exchange[2].wait_recv()
     ring_step(2, chip_term, ring_s, ring_r, arrived)
+    l_z(2)
+    l_y(-1, 1)
+    ring_step(3, chip_term, ring_s, ring_r, arrived)
+    l_over_y(3)
     l_z(3)
-    ring_step(3, chip_term, ring_s, ring_r, arrived)
-    l_y(-1, 1)
-    l_z(4)
 
     other, same = 2 * (1 - row) + k, 2 * row + k
     from_x = {}
@@ -218,6 +241,7 @@
         for side in (0, 1):
             from_x[side, h] = send(xs.at[h], xr.at[side, h], at_x(1 - 2 * side))
     l_y(-2, 2)
+    l_over_y(4)
     halves, passed = {}, []
     for h in (0, 1):
         for side in (0, 1):
@@ -228,16 +252,17 @@
             part = gt.at[other, pl.ds(64 * h + 32 * side, 32)]
             halves[side, h] = send(part, part, at_x(1 - 2 * side))
         passed.append(send(gt.at[other, rows], gt.at[other, rows], sibling))
-    l_y(-3, 3)
-    l_y(4)
     for h in (0, 1):
         for side in (0, 1):
             halves[side, h].wait_recv()
         rows = pl.ds(64 * h, 64)
         passed.append(send(gt.at[same, rows], gt.at[same, rows], sibling))
-    for n in (-1, 1, -2, 2, -3, 3, 4):
+    for n in (-1, 1, -2, 2):
         for sign in (1, -1):
             l_from["f", sign, n].wait_recv()
+    for n in (-3, 3, 4):
+        for sign in (1, -1, 2):
+            l_from["y", sign, n].wait_recv()
     for copy in passed:
         copy.wait_recv()
 
@@ -269,21 +294,21 @@
         return out.at[pl.ds(pl.multiple_of(start, 64), 64)]
 
     for h in (0, 1):
-        start = pl.multiple_of((xh * NZ + z) * 128 + k * 64 + h * 32, 32)
-        out[pl.ds(start, 32), :] = ring_end(h, partial, ring2_r, arrived2).astype(BF16)
+        final[h * 32:(h + 1) * 32, :] = ring_end(h, partial, ring2_r, arrived2).astype(BF16)
+    place = load(final, block(xh, 0))
 
     into, across = {}, []
 
-    def start_block(half):
-        for side in (0, 1):
-            into[half, side, 1] = send(block(xhs[half], 0), block(xhs[half], 0), at_z(1 - 2 * side))
-        across.append(send(block(xhs[half], 0), block(xhs[half], 0), sibling))
+    def start_block(half, src):
+        for side in (0, 1):
+            into[half, side, 1] = send(src, block(xhs[half], 0), at_z(1 - 2 * side))
+        across.append(send(src, block(xhs[half], 0), sibling))
 
     xhs = (xh, 1 - xh)
-    opposite = send(block(xh, 0), block(xh, 0), at_x(2))
-    start_block(0)
+    opposite = send(final, block(xh, 0), at_x(2))
+    start_block(0, final)
     opposite.wait_recv()
-    start_block(1)
+    start_block(1, block(1 - xh, 0))
     for step in range(1, 5):
         for half in (0, 1):
             for side in (0, 1):
@@ -298,6 +323,7 @@
                     across.append(send(block(xhs[half], n), block(xhs[half], n), sibling))
             if step == 4:
                 across.append(send(block(xhs[half], 4), block(xhs[half], 4), sibling))
+    place.wait()
     for copy in across:
         copy.wait_recv()
     for copy in sent:
@@ -307,13 +333,15 @@
 
 def shards(out_grads, activations, output_factor, input_factor):
     vmem = pltpu.VMEM
+    args = (out_grads, activations, output_factor, input_factor.T)
     dma = pltpu.SemaphoreType.DMA
     anywhere = pl.BlockSpec(memory_space=pl.ANY)
+    hbm = pl.BlockSpec(memory_space=pltpu.HBM)
     return pl.pallas_call(
         kernel,
-        out_shape=jax.ShapeDtypeStruct((2048, 1024), BF16),
-        in_specs=[anywhere] * 4,
-        out_specs=pl.BlockSpec(memory_space=pltpu.VMEM),
+        out_shape=pltpu.VMEM((2048, 1024), BF16),
+        in_specs=[hbm] * 4,
+        out_specs=anywhere,
         scratch_shapes=[
             vmem((1280, 2048), BF16),
             vmem((1280, 1024), BF16),
@@ -332,12 +360,13 @@
             vmem((8, 64, 1024), F32),
             vmem((2, 2, 4, 32, 1024), BF16),
             vmem((2, 2, 4, 32, 1024), BF16),
-            dma((8,)), dma((COPIES,)), dma((COPIES,)), dma((9,)), dma((9,)),
+            vmem((64, 1024), BF16),
+            dma((16,)), dma((COPIES,)), dma((COPIES,)), dma((9,)), dma((9,)),
         ],
         compiler_params=pltpu.CompilerParams(
-            collective_id=0, has_side_effects=True, vmem_limit_bytes=56 * 2**20
+            collective_id=0, has_side_effects=True, vmem_limit_bytes=40 * 2**20
         ),
-    )(out_grads, activations, output_factor, input_factor.T)
+    )(*(pltpu.with_memory_space_constraint(v, pltpu.HBM) for v in args))
 
 
 def solution(mesh):

time: 121 us -> 115 us (0.950)
  Pallas kernels: 116 us -> 113 us
  local copies, waits for them, and re-layouts: 4.64 us -> 2.02 us
    pallas_call x1, Pallas kernels: 116 us -> 113 us  [shards(): pl.pallas_call(kernel, out_shape=pltpu.VMEM((2048, 1024), BF16), in_specs...]
    unnamed x1, local copies, waits for them, and re-layouts: 4.64 us -> 2.02 us
where the time goes in v2:
time: 115 us
  Pallas kernels  113 us (98%)
  local copies, waits for them, and re-layouts  2.02 us (2%)
    pallas_call x1, Pallas kernels, shards(): pl.pallas_call(kernel, out_shape=pltpu.VMEM((2048, 1024), BF16), in_specs...  113 us

profile of v2, /device:TPU:1, one launch (start us, length us, event | category | flops | bytes accessed | tf_op | source)
XLA Modules:
  0.0 114.6 jit_solution(10930124983574377817)
XLA Ops:
  0.0 112.6 %shard_map.46 = bf16[2048,1024]{1,0:T(8,128)(2,1)S(1)} custom-call(bf16[1280,2048]{1,0:T(8,128)(2,1)} %g_hbm.1, bf16[1280,1024]{1,0:T(8,128)(2,1)} %a_hbm.1, bf16[1,64,4096]{2,1,0:T(8,128)(2,1)} %l_hbm.1, bf16[64,1024]{1,0:T(8,128)(2,1)} %bitcast.1), custom_call_target="tpu_custom_call" | custom-call | tf_op jit(solution)/shard_map/pallas_call | solution.py:340
  112.6 2.0 %copy.6 = bf16[2048,1024]{1,0:T(8,128)(2,1)} copy(bf16[2048,1024]{1,0:T(8,128)(2,1)S(1)} %shard_map.46) | data formatting | bytes 8388608

commit v3 on v2

v3 whole, which is shorter than its diff:
```python
import functools

import jax
import jax.numpy as jnp
from jax import lax
from jax.experimental import pallas as pl
from jax.experimental.pallas import tpu as pltpu
from jax.sharding import PartitionSpec as P

NX, NY, NZ = 4, 4, 8
BF16, F32 = jnp.bfloat16, jnp.float32
COPIES = 256


def kernel(
    g_hbm, a_hbm, l_hbm, r_hbm, out,
    g_v, a_v, own, give, take, cross_s, cross_r, ring_s, ring_r, gt, lbuf, rbuf, r_mine, mbuf, pf, far_s, far_r, ring2_s, ring2_r, final,
    load_sem, send_sem, recv_sem, r_send, r_recv,
):
    d, row, y = lax.axis_index("dp"), lax.axis_index("row"), lax.axis_index("col")
    k, z, xh = d % 2, (d // 2) % NZ, d // (2 * NZ)
    x = 2 * xh + row

    def device(x, y, z, k):
        return {"dp": (x // 2) * (2 * NZ) + z * 2 + k, "row": x % 2, "col": y}

    def at_x(n, core=None):
        return device((x + n) % NX, y, z, k if core is None else core)

    def at_y(n):
        return device(x, (y + n) % NY, z, k)

    def at_z(n):
        return device(x, y, (z + n) % NZ, k)

    sibling = device(x, y, z, 1 - k)
    count = [0]
    sent = []

    def send(src, dst, target):
        i = count[0]
        count[0] += 1
        copy = pltpu.make_async_remote_copy(
            src_ref=src, dst_ref=dst, send_sem=send_sem.at[i], recv_sem=recv_sem.at[i],
            device_id=target, device_id_type=pl.DeviceIdType.MESH,
        )
        copy.start()
        sent.append(copy)
        return copy

    loads = []

    def load(src, dst):
        copy = pltpu.make_async_copy(src, dst, load_sem.at[len(loads)])
        copy.start()
        loads.append(copy)
        return copy

    home = z // 4
    load_a = load(a_hbm, a_v)
    load_g = []
    for n in range(4):
        part = pl.ds(pl.multiple_of((n // 2 + (1 - k)) % 2 * 1024 + n % 2 * 512, 512), 512)
        load_g.append(load(g_hbm.at[:, part], g_v.at[:, part]))
    load_l = [load(l_hbm.at[0, :, pl.ds(q * 1024, 1024)], lbuf.at[q, z]) for q in range(4)]
    load_r = load(r_hbm, r_mine)

    barrier = pltpu.get_barrier_semaphore()
    partners = [at_z(1), at_z(-1), at_z(2), at_z(-2), at_z(4), sibling] + [at_y(n) for n in (1, 2, 3)]
    partners += [at_x(n, core) for n in (1, 2, 3) for core in (k, 1 - k)]
    for partner in partners:
        pl.semaphore_signal(barrier, inc=1, device_id=partner, device_id_type=pl.DeviceIdType.MESH)

    l_from = {}

    def l_block(q, n):
        return lbuf.at[q, (z + n) % NZ]

    def l_half(q, n, half):
        return lbuf.at[q, (z + n) % NZ, pl.ds(32 * half, 32)]

    def l_z(step):
        if step == 0:
            for sign in (1, -1):
                l_from[sign, 1] = send(l_block(y, 0), l_block(y, 0), at_z(sign))
            return
        for sign in (1, -1):
            n = -sign * step
            if step < 3:
                l_from[sign, step + 1] = send(l_block(y, n), l_block(y, n), at_z(sign))
            elif step == 3:
                half = 0 if sign == 1 else 1
                l_from[sign, 4] = send(l_half(y, n, half), l_half(y, n, half), at_z(sign))

    def l_over_y(step):
        for sign in (1, -1):
            l_from[sign, step].wait_recv()
        for n in ((-step, step) if step < 4 else (4,)):
            for sign in ((1, -1) if step < 4 else (1, -1, 2)):
                l_from["y", sign, n] = send(l_block(y, n), l_block(y, n), at_y(sign))

    def l_y(*offsets):
        for n in offsets:
            for sign in (1, -1):
                l_from["y", sign, n].wait_recv()
                half = 0 if sign == 1 else 1
                block = l_half((y + NY - sign) % NY, n, half)
                l_from["f", sign, n] = send(block, block, at_y(sign))

    def r_copy(src, dst, i, target):
        return pltpu.make_async_remote_copy(
            src_ref=src, dst_ref=dst, send_sem=r_send.at[i], recv_sem=r_recv.at[i],
            device_id=target, device_id_type=pl.DeviceIdType.MESH,
        )

    away = r_copy(r_mine, rbuf.at[2 * xh + home, row], 0, at_z(4))

    def pair(n):
        source = (x + NX - n) % NX
        return rbuf.at[pl.ds(source // 2 * 2, 2), source % 2]

    spread = [r_copy(pair(0), pair(0), n, at_x(n)) for n in (1, 2, 3)]
    handed = [r_copy(pair(n), pair(n), 4 + n, sibling) for n in range(4)]

    def r_x():
        @pl.when(k == home)
        def _():
            rbuf[2 * xh + home, row] = r_mine[...]
            away.wait_recv()
            for copy in spread:
                copy.start()
            handed[0].start()

    def r_core():
        @pl.when(k == home)
        def _():
            for n in (1, 2, 3):
                spread[n - 1].wait_recv()
                handed[n].start()

    def r_end():
        @pl.when(k == home)
        def _():
            for copy in spread + handed:
                copy.wait_send()

        @pl.when(k != home)
        def _():
            away.wait_send()
            for copy in handed:
                copy.wait_recv()

    exchange = {}

    def term(q_off, core):
        q = (z + q_off) % 4
        a_part = a_v[:, pl.ds(pl.multiple_of(q * 256, 256), 256)]

        def part(half, n):
            start = pl.multiple_of(half * 1024 + n * 512, 512)
            return lax.dot_general(
                a_part, g_v[:, pl.ds(start, 512)], (((0,), (0,)), ((), ())), preferred_element_type=F32
            )

        if core == 0:
            for n in range(2):
                give[q, :, n * 512:(n + 1) * 512] = part(1 - k, n).astype(BF16)
        else:
            for n in range(2):
                own[q, :, n * 512:(n + 1) * 512] = part(k, n)

    def trade(q_off):
        q = (z + q_off) % 4
        exchange[q_off] = send(give.at[q], take.at[q], sibling)

    cross = {}

    def chip_term(n, first, rows):
        chunk = (z + n) % NZ
        rows = pl.ds(pl.multiple_of((chunk // 4) * 128 + first, rows), rows)
        return own[chunk % 4, rows, :] + take[chunk % 4, rows, :].astype(F32)

    def cross_out(*offsets):
        for n in offsets:
            cross_s[n % NZ] = chip_term(n, (1 - xh) * 64, 64).astype(BF16)
            cross[n % NZ] = send(cross_s.at[n % NZ], cross_r.at[n % NZ], at_x(2))

    def half_term(n, h):
        return chip_term(n, xh * 64 + h * 32, 32) + cross_r[n % NZ, h * 32:(h + 1) * 32, :].astype(F32)

    def partial(n, h):
        return pf[h, (z + n) % NZ]

    arrived = {}

    def ring_step(step):
        for sign in (1, -1)[:1 if step == 0 else 2]:
            cross[sign * (4 - step) % NZ].wait_recv()
        for h, side in ((0, 0), (1, 1), (1, 0), (0, 1)):
            sign = 1 - 2 * side
            if step == 0 and h != side:
                continue
            total = half_term(sign * (4 - step), h)
            if (side, h) in arrived:
                arrived[side, h].wait_recv()
                total = total + ring_r[side, h, step - 1].astype(F32)
            ring_s[side, h, step] = total.astype(BF16)
            arrived[side, h] = send(ring_s.at[side, h, step], ring_r.at[side, h, step], at_z(sign))

    load_a.wait()
    for copy in load_g[:2]:
        copy.wait()
    term(0, 0)
    for copy in load_g[2:]:
        copy.wait()
    term(0, 1)
    term(3, 0)
    for copy in load_l:
        copy.wait()
    load_r.wait()
    pl.semaphore_wait(barrier, len(partners))
    trade(0)
    l_z(0)
    trade(3)

    @pl.when(k != home)
    def _():
        away.start()

    exchange[0].wait_recv()
    cross_out(4)
    term(1, 0)
    trade(1)
    term(3, 1)
    exchange[3].wait_recv()
    cross_out(3)
    term(1, 1)
    exchange[1].wait_recv()
    cross_out(-3)
    l_over_y(1)
    l_z(1)
    term(2, 0)
    trade(2)
    ring_step(0)
    term(2, 1)
    exchange[2].wait_recv()
    cross_out(2, -2, 1, -1, 0)
    l_over_y(2)
    l_z(2)
    ring_step(1)
    l_y(-1, 1)
    ring_step(2)
    l_over_y(3)
    l_z(3)
    ring_step(3)
    r_x()
    l_y(-2, 2)
    l_over_y(4)

    def piece_of(n):
        source = (x + NX - n) % NX
        return gt.at[2 * (source % 2) + k, pl.ds(pl.multiple_of(source // 2 * 64, 64), 64)]

    cross[0].wait_recv()
    for h in (0, 1):
        for side in (0, 1):
            arrived[side, h].wait_recv()
        rows = pl.ds(pl.multiple_of(xh * 64 + h * 32, 32), 32)
        gt[2 * row + k, rows, :] = (
            half_term(0, h) + ring_r[0, h, 3].astype(F32) + ring_r[1, h, 3].astype(F32)
        ).astype(BF16)
    from_x = {n: send(piece_of(0), piece_of(0), at_x(n)) for n in (1, 3, 2)}
    passed = [send(piece_of(0), piece_of(0), sibling)]
    l_y(-3, 3)
    for n in (1, 3, 2):
        from_x[n].wait_recv()
        passed.append(send(piece_of(n), piece_of(n), sibling))
    r_core()
    for n in (-1, 1, -2, 2, -3, 3):
        for sign in (1, -1):
            l_from["f", sign, n].wait_recv()
    for sign in (1, -1, 2):
        l_from["y", sign, 4].wait_recv()
    for copy in passed:
        copy.wait_recv()

    gathered = {}
    for h in (0, 1):
        left = jnp.zeros((128, 256), F32)
        for q in range(4):
            left = left + lax.dot_general(
                gt[q], lbuf[q, :, h * 32:(h + 1) * 32, :].reshape(256, 1024), (((1,), (1,)), ((), ())),
                preferred_element_type=F32,
            )
        mbuf[h, y] = left.astype(BF16)
        gathered[h] = [send(mbuf.at[h, y], mbuf.at[h, y], at_y(n)) for n in (1, 3, 2)]
    r_end()

    met, far = {}, {}

    def sum_start(h):
        for side in (0, 1):
            sign = 1 - 2 * side
            if h == side:
                far_s[side] = partial(sign * 4, h).astype(BF16)
                far[side] = send(far_s.at[side], far_r.at[side], at_z(2 * sign))
            ring2_s[side, h, 0] = partial(sign * 3, h).astype(BF16)
            met[side, h] = send(ring2_s.at[side, h, 0], ring2_r.at[side, h, 0], at_z(sign))

    def sum_step(step, h):
        for side in (0, 1):
            sign = 1 - 2 * side
            total = partial(sign * (3 - step), h)
            met[side, h].wait_recv()
            total = total + ring2_r[side, h, step - 1].astype(F32)
            if step == 1 and h == side:
                far[side].wait_recv()
                total = total + far_r[side].astype(F32)
            ring2_s[side, h, step] = total.astype(BF16)
            met[side, h] = send(ring2_s.at[side, h, step], ring2_r.at[side, h, step], at_z(sign))

    for h in (0, 1):
        for copy in gathered[h]:
            copy.wait_recv()
        left_all = mbuf[h].reshape(512, 256)
        for n in range(2):
            right = rbuf[:, :, :, n * 512:(n + 1) * 512].reshape(512, 512)
            pf[h, :, :, n * 512:(n + 1) * 512] = lax.dot_general(
                left_all, right, (((0,), (0,)), ((), ())), preferred_element_type=F32
            ).reshape(8, 32, 512)
        sum_start(h)
    for step in (1, 2):
        for h in (0, 1):
            sum_step(step, h)

    def block(half, n, first=0, rows=64):
        start = (half * NZ + (z + n) % NZ) * 128 + k * 64 + first
        return out.at[pl.ds(pl.multiple_of(start, 16), rows)]

    into, across, crossed = {}, [], {}
    near, away_half = xh, 1 - xh

    def step_out(half, h, side, step):
        sign = 1 - 2 * side
        n = -sign * (step - 1)
        piece = block(half, n, 32 * h, 32)
        into[half is near, h, side, step] = send(piece, piece, at_z(sign))
        if step == 3:
            quarter = block(half, n, 32 * h + 16 * side, 16)
            into[half is near, h, side, 4] = send(quarter, quarter, at_z(2 * sign))

    def over_x(n):
        piece = block(near, n, 32, 32)
        crossed[n] = send(piece, piece, at_x(2))

    def over_core(half, n, first=0, rows=64):
        piece = block(half, n, first, rows)
        across.append(send(piece, piece, sibling))

    for h in (1, 0):
        for side in (0, 1):
            met[side, h].wait_recv()
        rows = slice(h * 32, (h + 1) * 32)
        final[rows, :] = (
            partial(0, h) + ring2_r[0, h, 2].astype(F32) + ring2_r[1, h, 2].astype(F32)
        ).astype(BF16)
        place = load(final.at[pl.ds(h * 32, 32)], block(near, 0, 32 * h, 32))
        place.wait()
        if h == 0:
            crossed["h0"] = send(block(near, 0, 0, 32), block(near, 0, 0, 32), at_x(2))
        for side in (0, 1):
            step_out(near, h, side, 1)
        if h == 1:
            over_x(0)
    over_core(near, 0)

    def own_class(step):
        for h in (1, 0):
            for side in (0, 1):
                into[True, h, side, step].wait_recv()
                if step < 3:
                    step_out(near, h, side, step + 1)
                if h == 1 and step < 4:
                    over_x((2 * side - 1) * step)
            if h == 1 and step == 4:
                over_x(4)
        for n in ((-step, step) if step < 4 else (4,)):
            over_core(near, n)

    def opposite(step):
        for side in (0, 1):
            into[False, 0, side, step].wait_recv()
            if step < 3:
                step_out(away_half, 0, side, step + 1)
        for n in ((-step, step) if step < 4 else (4,)):
            over_core(away_half, n, 0, 32)

    def from_opposite(*offsets):
        for n in offsets:
            crossed[n].wait_recv()
            over_core(away_half, n, 32, 32)

    own_class(1)
    crossed["h0"].wait_recv()
    for side in (0, 1):
        step_out(away_half, 0, side, 1)
    over_core(away_half, 0, 0, 32)
    own_class(2)
    from_opposite(0)
    opposite(1)
    from_opposite(-1, 1)
    own_class(3)
    own_class(4)
    opposite(2)
    from_opposite(-2, 2)
    opposite(3)
    opposite(4)
    from_opposite(-3, 3, 4)
    for copy in across:
        copy.wait_recv()
    for copy in sent:
        copy.wait_send()
    assert count[0] <= COPIES, count[0]


def shards(out_grads, activations, output_factor, input_factor):
    vmem = pltpu.VMEM
    args = (out_grads, activations, output_factor, input_factor.T)
    dma = pltpu.SemaphoreType.DMA
    anywhere = pl.BlockSpec(memory_space=pl.ANY)
    hbm = pl.BlockSpec(memory_space=pltpu.HBM)
    return pl.pallas_call(
        kernel,
        out_shape=pltpu.VMEM((2048, 1024), BF16),
        in_specs=[hbm] * 4,
        out_specs=anywhere,
        scratch_shapes=[
            vmem((1280, 2048), BF16),
            vmem((1280, 1024), BF16),
            vmem((4, 256, 1024), F32),
            vmem((4, 256, 1024), BF16),
            vmem((4, 256, 1024), BF16),
            vmem((8, 64, 1024), BF16),
            vmem((8, 64, 1024), BF16),
            vmem((2, 2, 4, 32, 1024), BF16),
            vmem((2, 2, 4, 32, 1024), BF16),
            vmem((4, 128, 1024), BF16),
            vmem((4, 8, 64, 1024), BF16),
            vmem((4, 2, 64, 1024), BF16),
            vmem((64, 1024), BF16),
            vmem((2, 4, 128, 256), BF16),
            vmem((2, 8, 32, 1024), F32),
            vmem((2, 32, 1024), BF16),
            vmem((2, 32, 1024), BF16),
            vmem((2, 2, 3, 32, 1024), BF16),
            vmem((2, 2, 3, 32, 1024), BF16),
            vmem((64, 1024), BF16),
            dma((16,)), dma((COPIES,)), dma((COPIES,)), dma((9,)), dma((9,)),
        ],
        compiler_params=pltpu.CompilerParams(
            collective_id=0, has_side_effects=True, vmem_limit_bytes=40 * 2**20
        ),
    )(*(pltpu.with_memory_space_constraint(v, pltpu.HBM) for v in args))


def solution(mesh):
    placed = (P("dp", "row"), P("dp", "col"), P("row", "dp", None), P("col", ("dp", "row")))
    return jax.shard_map(
        shards, mesh=mesh, in_specs=placed, out_specs=P("row", "col"), check_vma=False
    )
```

time: 115 us -> 105 us (0.913)
  Pallas kernels: 113 us -> 103 us
    pallas_call x1, Pallas kernels: 113 us -> 103 us  [shards(): pl.pallas_call(kernel, out_shape=pltpu.VMEM((2048, 1024), BF16), in_specs...]
where the time goes in v3:
time: 105 us
  Pallas kernels  103 us (98%)
  local copies, waits for them, and re-layouts  2.02 us (2%)
    pallas_call x1, Pallas kernels, shards(): pl.pallas_call(kernel, out_shape=pltpu.VMEM((2048, 1024), BF16), in_specs...  103 us

profile of v3, /device:TPU:1, one launch (start us, length us, event | category | flops | bytes accessed | tf_op | source)
XLA Modules:
  0.0 105.2 jit_solution(9202769821888058502)
XLA Ops:
  0.0 103.1 %shard_map.46 = bf16[2048,1024]{1,0:T(8,128)(2,1)S(1)} custom-call(bf16[1280,2048]{1,0:T(8,128)(2,1)} %g_hbm.1, bf16[1280,1024]{1,0:T(8,128)(2,1)} %a_hbm.1, bf16[1,64,4096]{2,1,0:T(8,128)(2,1)} %l_hbm.1, bf16[64,1024]{1,0:T(8,128)(2,1)} %bitcast.1), custom_call_target="tpu_custom_call" | custom-call | tf_op jit(solution)/shard_map/pallas_call | solution.py:432
  103.2 2.0 %copy.6 = bf16[2048,1024]{1,0:T(8,128)(2,1)} copy(bf16[2048,1024]{1,0:T(8,128)(2,1)S(1)} %shard_map.46) | data formatting | bytes 8388608

commit v4 on v3

--- a/solution.py
+++ b/solution.py
@@ -9,7 +9,7 @@
 
 NX, NY, NZ = 4, 4, 8
 BF16, F32 = jnp.bfloat16, jnp.float32
-COPIES = 256
+COPIES = 146
 
 
 def kernel(
@@ -48,6 +48,11 @@
         sent.append(copy)
         return copy
 
+    def retire(count):
+        for copy in sent[:count]:
+            copy.wait_send()
+        del sent[:count]
+
     loads = []
 
     def load(src, dst):
@@ -57,11 +62,18 @@
         return copy
 
     home = z // 4
-    load_a = load(a_hbm, a_v)
-    load_g = []
+    load_a, load_g = {}, []
+
+    def load_columns(n):
+        part = pl.ds(pl.multiple_of((z + n) % 4 * 256, 256), 256)
+        load_a[n] = load(a_hbm.at[:, part], a_v.at[:, part])
+
+    load_columns(0)
     for n in range(4):
         part = pl.ds(pl.multiple_of((n // 2 + (1 - k)) % 2 * 1024 + n % 2 * 512, 512), 512)
         load_g.append(load(g_hbm.at[:, part], g_v.at[:, part]))
+    for n in (3, 1, 2):
+        load_columns(n)
     load_l = [load(l_hbm.at[0, :, pl.ds(q * 1024, 1024)], lbuf.at[q, z]) for q in range(4)]
     load_r = load(r_hbm, r_mine)
 
@@ -119,15 +131,30 @@
         source = (x + NX - n) % NX
         return rbuf.at[pl.ds(source // 2 * 2, 2), source % 2]
 
-    spread = [r_copy(pair(0), pair(0), n, at_x(n)) for n in (1, 2, 3)]
-    handed = [r_copy(pair(n), pair(n), 4 + n, sibling) for n in range(4)]
-
-    def r_x():
+    def slot(source, n):
+        return rbuf.at[2 * (source // 2) + n, source % 2]
+
+    own_spread = [r_copy(r_mine, slot(x, home), n, at_x(n)) for n in (1, 2, 3)]
+    far_spread = [r_copy(slot(x, 1 - home), slot(x, 1 - home), 3 + n, at_x(n)) for n in (1, 2, 3)]
+    handed = [r_copy(pair(n), pair(n), 7 + n, sibling) for n in range(4)]
+
+    def r_first():
         @pl.when(k == home)
         def _():
+            for copy in own_spread:
+                copy.start()
             rbuf[2 * xh + home, row] = r_mine[...]
+
+    def r_away():
+        @pl.when(k != home)
+        def _():
+            away.start()
+
+    def r_second():
+        @pl.when(k == home)
+        def _():
             away.wait_recv()
-            for copy in spread:
+            for copy in far_spread:
                 copy.start()
             handed[0].start()
 
@@ -135,13 +162,14 @@
         @pl.when(k == home)
         def _():
             for n in (1, 2, 3):
-                spread[n - 1].wait_recv()
+                own_spread[n - 1].wait_recv()
+                far_spread[n - 1].wait_recv()
                 handed[n].start()
 
     def r_end():
         @pl.when(k == home)
         def _():
-            for copy in spread + handed:
+            for copy in own_spread + far_spread + handed:
                 copy.wait_send()
 
         @pl.when(k != home)
@@ -207,28 +235,27 @@
             ring_s[side, h, step] = total.astype(BF16)
             arrived[side, h] = send(ring_s.at[side, h, step], ring_r.at[side, h, step], at_z(sign))
 
-    load_a.wait()
+    load_a[0].wait()
     for copy in load_g[:2]:
         copy.wait()
     term(0, 0)
-    for copy in load_g[2:]:
-        copy.wait()
-    term(0, 1)
-    term(3, 0)
     for copy in load_l:
         copy.wait()
     load_r.wait()
     pl.semaphore_wait(barrier, len(partners))
     trade(0)
     l_z(0)
+    r_first()
+    for copy in load_g[2:]:
+        copy.wait()
+    term(0, 1)
+    load_a[3].wait()
+    term(3, 0)
     trade(3)
-
-    @pl.when(k != home)
-    def _():
-        away.start()
-
     exchange[0].wait_recv()
     cross_out(4)
+    load_a[1].wait()
+    load_a[2].wait()
     term(1, 0)
     trade(1)
     term(3, 1)
@@ -242,6 +269,7 @@
     term(2, 0)
     trade(2)
     ring_step(0)
+    r_away()
     term(2, 1)
     exchange[2].wait_recv()
     cross_out(2, -2, 1, -1, 0)
@@ -249,13 +277,14 @@
     l_z(2)
     ring_step(1)
     l_y(-1, 1)
+    retire(12)
     ring_step(2)
     l_over_y(3)
     l_z(3)
     ring_step(3)
-    r_x()
     l_y(-2, 2)
     l_over_y(4)
+    retire(30)
 
     def piece_of(n):
         source = (x + NX - n) % NX
@@ -275,7 +304,7 @@
     for n in (1, 3, 2):
         from_x[n].wait_recv()
         passed.append(send(piece_of(n), piece_of(n), sibling))
-    r_core()
+    r_second()
     for n in (-1, 1, -2, 2, -3, 3):
         for sign in (1, -1):
             l_from["f", sign, n].wait_recv()
@@ -294,6 +323,8 @@
             )
         mbuf[h, y] = left.astype(BF16)
         gathered[h] = [send(mbuf.at[h, y], mbuf.at[h, y], at_y(n)) for n in (1, 3, 2)]
+    r_core()
+    retire(len(sent) - 10)
     r_end()
 
     met, far = {}, {}
@@ -357,22 +388,26 @@
         piece = block(half, n, first, rows)
         across.append(send(piece, piece, sibling))
 
+    def mine(h):
+        return final.at[pl.ds(h * 32, 32)], block(near, 0, 32 * h, 32)
+
+    places = []
+    for h in (0, 1):
+        for side in (0, 1):
+            met[side, h].wait_recv()
+        final[h * 32:(h + 1) * 32, :] = (
+            partial(0, h) + ring2_r[0, h, 2].astype(F32) + ring2_r[1, h, 2].astype(F32)
+        ).astype(BF16)
+        if h == 0:
+            crossed["h0"] = send(*mine(0), at_x(2))
+        places.append(load(*mine(h)))
     for h in (1, 0):
         for side in (0, 1):
-            met[side, h].wait_recv()
-        rows = slice(h * 32, (h + 1) * 32)
-        final[rows, :] = (
-            partial(0, h) + ring2_r[0, h, 2].astype(F32) + ring2_r[1, h, 2].astype(F32)
-        ).astype(BF16)
-        place = load(final.at[pl.ds(h * 32, 32)], block(near, 0, 32 * h, 32))
-        place.wait()
-        if h == 0:
-            crossed["h0"] = send(block(near, 0, 0, 32), block(near, 0, 0, 32), at_x(2))
-        for side in (0, 1):
-            step_out(near, h, side, 1)
+            into[True, h, side, 1] = send(*mine(h), at_z(1 - 2 * side))
         if h == 1:
-            over_x(0)
-    over_core(near, 0)
+            crossed[0] = send(*mine(1), at_x(2))
+    for h in (0, 1):
+        across.append(send(*mine(h), sibling))
 
     def own_class(step):
         for h in (1, 0):
@@ -400,6 +435,7 @@
             crossed[n].wait_recv()
             over_core(away_half, n, 32, 32)
 
+    retire(len(sent) - 16)
     own_class(1)
     crossed["h0"].wait_recv()
     for side in (0, 1):
@@ -409,18 +445,23 @@
     from_opposite(0)
     opposite(1)
     from_opposite(-1, 1)
+    retire(len(sent) - 34)
     own_class(3)
     own_class(4)
+    retire(len(sent) - 34)
     opposite(2)
     from_opposite(-2, 2)
     opposite(3)
     opposite(4)
     from_opposite(-3, 3, 4)
+    retire(len(sent) - 14)
+    for copy in places:
+        copy.wait()
     for copy in across:
         copy.wait_recv()
     for copy in sent:
         copy.wait_send()
-    assert count[0] <= COPIES, count[0]
+    assert count[0] == COPIES, count[0]
 
 
 def shards(out_grads, activations, output_factor, input_factor):
@@ -455,7 +496,7 @@
             vmem((2, 2, 3, 32, 1024), BF16),
             vmem((2, 2, 3, 32, 1024), BF16),
             vmem((64, 1024), BF16),
-            dma((16,)), dma((COPIES,)), dma((COPIES,)), dma((9,)), dma((9,)),
+            dma((16,)), dma((COPIES,)), dma((COPIES,)), dma((11,)), dma((11,)),
         ],
         compiler_params=pltpu.CompilerParams(
             collective_id=0, has_side_effects=True, vmem_limit_bytes=40 * 2**20

time: 105 us -> 102 us (0.971)
  Pallas kernels: 103 us -> 99.8 us
    pallas_call x1, Pallas kernels: 103 us -> 99.8 us  [shards(): pl.pallas_call(kernel, out_shape=pltpu.VMEM((2048, 1024), BF16), in_specs...]
where the time goes in v4:
time: 102 us
  Pallas kernels  99.8 us (98%)
  local copies, waits for them, and re-layouts  2.02 us (2%)
    pallas_call x1, Pallas kernels, shards(): pl.pallas_call(kernel, out_shape=pltpu.VMEM((2048, 1024), BF16), in_specs...  99.8 us

profile of v4, /device:TPU:1, one launch (start us, length us, event | category | flops | bytes accessed | tf_op | source)
XLA Modules:
  0.0 101.9 jit_solution(13856819955189249891)
XLA Ops:
  0.0 99.8 %shard_map.46 = bf16[2048,1024]{1,0:T(8,128)(2,1)S(1)} custom-call(bf16[1280,2048]{1,0:T(8,128)(2,1)} %g_hbm.1, bf16[1280,1024]{1,0:T(8,128)(2,1)} %a_hbm.1, bf16[1,64,4096]{2,1,0:T(8,128)(2,1)} %l_hbm.1, bf16[64,1024]{1,0:T(8,128)(2,1)} %bitcast.1), custom_call_target="tpu_custom_call" | custom-call | tf_op jit(solution)/shard_map/pallas_call | solution.py:473
  99.8 2.0 %copy.6 = bf16[2048,1024]{1,0:T(8,128)(2,1)} copy(bf16[2048,1024]{1,0:T(8,128)(2,1)S(1)} %shard_map.46) | data formatting | bytes 8388608

commit v5 on v4

--- a/solution.py
+++ b/solution.py
@@ -245,7 +245,6 @@
     pl.semaphore_wait(barrier, len(partners))
     trade(0)
     l_z(0)
-    r_first()
     for copy in load_g[2:]:
         copy.wait()
     term(0, 1)
@@ -268,11 +267,13 @@
     l_z(1)
     term(2, 0)
     trade(2)
+    term(2, 1)
+    exchange[2].wait_recv()
+    cross_out(2, -2)
     ring_step(0)
     r_away()
-    term(2, 1)
-    exchange[2].wait_recv()
-    cross_out(2, -2, 1, -1, 0)
+    cross_out(1, -1, 0)
+    r_first()
     l_over_y(2)
     l_z(2)
     ring_step(1)
@@ -298,7 +299,7 @@
         gt[2 * row + k, rows, :] = (
             half_term(0, h) + ring_r[0, h, 3].astype(F32) + ring_r[1, h, 3].astype(F32)
         ).astype(BF16)
-    from_x = {n: send(piece_of(0), piece_of(0), at_x(n)) for n in (1, 3, 2)}
+    from_x = {n: send(piece_of(0), piece_of(0), at_x(n)) for n in (2, 1, 3)}
     passed = [send(piece_of(0), piece_of(0), sibling)]
     l_y(-3, 3)
     for n in (1, 3, 2):
@@ -322,7 +323,7 @@
                 preferred_element_type=F32,
             )
         mbuf[h, y] = left.astype(BF16)
-        gathered[h] = [send(mbuf.at[h, y], mbuf.at[h, y], at_y(n)) for n in (1, 3, 2)]
+        gathered[h] = [send(mbuf.at[h, y], mbuf.at[h, y], at_y(n)) for n in (2, 1, 3)]
     r_core()
     retire(len(sent) - 10)
     r_end()
@@ -409,25 +410,27 @@
     for h in (0, 1):
         across.append(send(*mine(h), sibling))
 
-    def own_class(step):
-        for h in (1, 0):
-            for side in (0, 1):
-                into[True, h, side, step].wait_recv()
-                if step < 3:
-                    step_out(near, h, side, step + 1)
-                if h == 1 and step < 4:
-                    over_x((2 * side - 1) * step)
-            if h == 1 and step == 4:
-                over_x(4)
-        for n in ((-step, step) if step < 4 else (4,)):
-            over_core(near, n)
+    def around(step):
+        return (-step, step) if step < 4 else (4,)
+
+    def own_class(h, step):
+        for side in (0, 1):
+            into[True, h, side, step].wait_recv()
+            if step < 3:
+                step_out(near, h, side, step + 1)
+        if h == 1:
+            for n in around(step):
+                over_x(n)
+        else:
+            for n in around(step):
+                over_core(near, n)
 
     def opposite(step):
         for side in (0, 1):
             into[False, 0, side, step].wait_recv()
             if step < 3:
                 step_out(away_half, 0, side, step + 1)
-        for n in ((-step, step) if step < 4 else (4,)):
+        for n in around(step):
             over_core(away_half, n, 0, 32)
 
     def from_opposite(*offsets):
@@ -436,24 +439,28 @@
             over_core(away_half, n, 32, 32)
 
     retire(len(sent) - 16)
-    own_class(1)
+    own_class(1, 1)
     crossed["h0"].wait_recv()
     for side in (0, 1):
         step_out(away_half, 0, side, 1)
+    own_class(0, 1)
     over_core(away_half, 0, 0, 32)
-    own_class(2)
     from_opposite(0)
+    own_class(1, 2)
     opposite(1)
+    own_class(0, 2)
     from_opposite(-1, 1)
     retire(len(sent) - 34)
-    own_class(3)
-    own_class(4)
-    retire(len(sent) - 34)
+    own_class(1, 3)
     opposite(2)
+    own_class(1, 4)
+    own_class(0, 3)
     from_opposite(-2, 2)
     opposite(3)
+    own_class(0, 4)
+    from_opposite(-3, 3)
     opposite(4)
-    from_opposite(-3, 3, 4)
+    from_opposite(4)
     retire(len(sent) - 14)
     for copy in places:
         copy.wait()

time: 102 us -> 98.4 us (0.965)
  Pallas kernels: 99.8 us -> 96.3 us
    pallas_call x1, Pallas kernels: 99.8 us -> 96.3 us  [shards(): pl.pallas_call(kernel, out_shape=pltpu.VMEM((2048, 1024), BF16), in_specs...]
where the time goes in v5:
time: 98.4 us; the launch traced here: 98.3 us
  Pallas kernels  96.3 us (98%)
  local copies, waits for them, and re-layouts  2.02 us (2%)
    pallas_call x1, Pallas kernels, shards(): pl.pallas_call(kernel, out_shape=pltpu.VMEM((2048, 1024), BF16), in_specs...  96.3 us
    unnamed x1, local copies, waits for them, and re-layouts  2.02 us

profile of v5, /device:TPU:1, one launch (start us, length us, event | category | flops | bytes accessed | tf_op | source)
XLA Modules:
  0.0 98.3 jit_solution(7358841608245933152)
XLA Ops:
  0.0 96.3 %shard_map.46 = bf16[2048,1024]{1,0:T(8,128)(2,1)S(1)} custom-call(bf16[1280,2048]{1,0:T(8,128)(2,1)} %g_hbm.1, bf16[1280,1024]{1,0:T(8,128)(2,1)} %a_hbm.1, bf16[1,64,4096]{2,1,0:T(8,128)(2,1)} %l_hbm.1, bf16[64,1024]{1,0:T(8,128)(2,1)} %bitcast.1), custom_call_target="tpu_custom_call" | custom-call | tf_op jit(solution)/shard_map/pallas_call | solution.py:480
  96.3 2.0 %copy.6 = bf16[2048,1024]{1,0:T(8,128)(2,1)} copy(bf16[2048,1024]{1,0:T(8,128)(2,1)S(1)} %shard_map.46) | data formatting | bytes 8388608

commit v6 on v5

--- a/solution.py
+++ b/solution.py
@@ -331,16 +331,16 @@
     met, far = {}, {}
 
     def sum_start(h):
-        for side in (0, 1):
+        sign = 1 - 2 * h
+        far_s[h] = partial(sign * 4, h).astype(BF16)
+        far[h] = send(far_s.at[h], far_r.at[h], at_z(2 * sign))
+        for side in (h, 1 - h):
             sign = 1 - 2 * side
-            if h == side:
-                far_s[side] = partial(sign * 4, h).astype(BF16)
-                far[side] = send(far_s.at[side], far_r.at[side], at_z(2 * sign))
             ring2_s[side, h, 0] = partial(sign * 3, h).astype(BF16)
             met[side, h] = send(ring2_s.at[side, h, 0], ring2_r.at[side, h, 0], at_z(sign))
 
     def sum_step(step, h):
-        for side in (0, 1):
+        for side in (1 - h, h):
             sign = 1 - 2 * side
             total = partial(sign * (3 - step), h)
             met[side, h].wait_recv()

time: 98.4 us -> 98 us (level)
  no operation moved by 1% of the time
where the time goes in v6:
time: 98 us; the launch traced here: 97.9 us
  Pallas kernels  95.9 us (98%)
  local copies, waits for them, and re-layouts  2.02 us (2%)
    pallas_call x1, Pallas kernels, shards(): pl.pallas_call(kernel, out_shape=pltpu.VMEM((2048, 1024), BF16), in_specs...  95.9 us
    unnamed x1, local copies, waits for them, and re-layouts  2.02 us

profile of v6, /device:TPU:1, one launch (start us, length us, event | category | flops | bytes accessed | tf_op | source)
XLA Modules:
  0.0 97.9 jit_solution(11040866271706055786)
XLA Ops:
  0.0 95.9 %shard_map.46 = bf16[2048,1024]{1,0:T(8,128)(2,1)S(1)} custom-call(bf16[1280,2048]{1,0:T(8,128)(2,1)} %g_hbm.1, bf16[1280,1024]{1,0:T(8,128)(2,1)} %a_hbm.1, bf16[1,64,4096]{2,1,0:T(8,128)(2,1)} %l_hbm.1, bf16[64,1024]{1,0:T(8,128)(2,1)} %bitcast.1), custom_call_target="tpu_custom_call" | custom-call | tf_op jit(solution)/shard_map/pallas_call | solution.py:480
  95.9 2.0 %copy.6 = bf16[2048,1024]{1,0:T(8,128)(2,1)} copy(bf16[2048,1024]{1,0:T(8,128)(2,1)S(1)} %shard_map.46) | data formatting | bytes 8388608
